TPU v7x, 32 devices: a whole 2x2x4 slice. The times are simulated.
32 devices in a mesh: blk: 16 (over z, x, core), pair: 2 (over y).
Axes of the slice: x: 2, y: 2, z: 4, core: 2. Of those that a mesh axis runs over, the one named last changes fastest.
Arguments:
- images: bfloat16 [14336, 768], P(('blk', 'pair')), may hold values from -1 to 1
- texts: bfloat16 [14336, 768], P(('blk', 'pair')), may hold values from -1 to 1
- scale: float32 [], replicated, may hold values from 4 to 16
- bias: float32 [], replicated, may hold values from -6 to -2
Outputs:
- row_loss: float32 [14336], P(('blk', 'pair'))
- grad_images: float32 [14336, 768], P(('blk', 'pair'))
- grad_texts: float32 [14336, 768], P(('blk', 'pair'))
All inputs are finite; a program needn't handle non-finite values.
Results may differ from a plain program's by a relative error of at most 0.0056.
Values may be sent and summed in bfloat16 or wider, within the bound.
A program may use at most 128 MiB of HBM per device.

v0:
```python
import jax
import jax.numpy as jnp
from jax import lax
from jax.sharding import PartitionSpec as P

STEPS = 6


EPSILON = 1e-06


def passed_along(block, axis, distance):
    devices = range(lax.axis_size(axis))
    route = [((i - distance) % len(devices), i) for i in devices]
    return lax.ppermute(block, axis, route)


def unit_rows(features):
    widened = features.astype(jnp.float32)
    inverse = lax.rsqrt(jnp.sum(widened * widened, axis=1, keepdims=True) + EPSILON)
    return (widened * inverse, inverse)


def tangent(unit, inverse, direction):
    return inverse * (direction - unit * jnp.sum(unit * direction, axis=1, keepdims=True))


def make_labels(logits, offset, row_count):
    if offset == 0:
        column = lax.broadcasted_iota(jnp.int32, logits.shape, 1)
        target = (
            lax.broadcasted_iota(jnp.int32, logits.shape, 0) + lax.axis_index("pair") * row_count
        )
        return jnp.where(column == target, 1.0, -1.0).astype(jnp.float32)
    return -1.0


def move_partials(partial_rows, steps_by):
    return passed_along(partial_rows, "blk", steps_by)


def visit(image_emb, text_now, offset, scale, bias):
    logits = (
        scale
        * lax.dot_general(
            image_emb, text_now, (((1,), (1,)), ((), ())), preferred_element_type=jnp.float32
        )
        + bias
    )
    labels = make_labels(logits, offset, image_emb.shape[0])
    margin = labels * logits
    loss_rows = jnp.sum(jax.nn.softplus(-margin), axis=1)
    weights_bf = (scale * -labels * jax.nn.sigmoid(-margin)).astype(jnp.bfloat16)
    image_grad = jnp.dot(weights_bf, text_now, preferred_element_type=jnp.float32)
    text_grad = None
    text_grad = lax.dot_general(
        weights_bf, image_emb, (((0,), (0,)), ((), ())), preferred_element_type=jnp.float32
    )
    text_grad = lax.psum_scatter(text_grad, "pair", scatter_dimension=0, tiled=True)
    return (loss_rows, image_grad, text_grad)


def body(images, texts, scale, bias):
    image_unit, image_inverse = unit_rows(images)
    text_unit, text_inverse = unit_rows(texts)
    image_emb = image_unit.astype(jnp.bfloat16)
    text_emb = text_unit.astype(jnp.bfloat16)
    text_now = lax.all_gather(text_emb, "pair", axis=0, tiled=True)
    loss_total = jnp.zeros((images.shape[0],), jnp.float32)
    image_dir = jnp.zeros(images.shape, jnp.float32)
    partial_value = None
    for offset in range(STEPS):
        next_text = passed_along(text_now, "blk", 1) if offset + 1 < STEPS else text_now
        loss_rows, image_grad, text_grad = visit(image_emb, text_now, offset, scale, bias)
        loss_total = loss_total + loss_rows
        image_dir = image_dir + image_grad
        partial_value = text_grad if offset == 0 else partial_value + text_grad
        if offset + 1 < STEPS:
            partial_value = move_partials(partial_value, 1)
        text_now = next_text
    partial_value = move_partials(partial_value, 1 - STEPS)
    window = STEPS * lax.axis_size("pair") * images.shape[0]
    row_loss = loss_total / window
    grad_images = tangent(image_unit, image_inverse, image_dir)
    grad_texts = tangent(text_unit, text_inverse, partial_value)
    return (row_loss, grad_images, grad_texts)


def solution(mesh):
    in_specs = (P(("blk", "pair"), None), P(("blk", "pair"), None), P(), P())
    out_specs = (P(("blk", "pair")), P(("blk", "pair"), None), P(("blk", "pair"), None))
    return jax.shard_map(body, mesh=mesh, in_specs=in_specs, out_specs=out_specs, check_vma=False)
```

profile of v0, /device:TPU:27, one launch (start us, length us, event | category | flops | bytes accessed | tf_op | source)
XLA Modules:
  0.0 348.8 jit_solution(16768228295773016830)
XLA Ops:
  12.3 24.5 %all-gather.2.cloned.1.call-done = bf16[896,768]{1,0:T(8,128)(2,1)} async-done(((bf16[448,768]{1,0:T(8,128)(2,1)}), bf16[896,768]{1,0:T(8,128)(2,1)}) %all-gather.2.cloned.1.call-update) | async-done | bytes 1376272 | tf_op jit(solution)/shard_map/all_gather | solution.py:68
  36.9 3.6 %fusion.8 = (bf16[448,896]{1,0:T(8,128)(2,1)S(1)}, f32[448]{0:T(512)S(1)}) fusion(f32[]{:T(128)S(6)} %copy.7, s32[448]{0:T(512)S(1)} %iota_add_fusion, f32[]{:T(128)S(6)} %copy.8, bf16[896,768]{1,0:T(8,128)(2,1)} %all-gather.2.cloned.1.call-done, bf16[448,768]{1,0:T(8,128)(2,1)S(1)} %copy-done.1, f32[448]{0:T(512)S(1)} %add_rsqrt_fusion.1), kind=kOutput, calls=%fused_computation.20 | convolution fusion | flops 625221184 | bytes 2872584 | tf_op jit(solution)/shard_map/dot_general | solution.py:45
  46.0 15.3 %collective-permute-done = bf16[896,768]{1,0:T(8,128)(2,1)S(1)} collective-permute-done((bf16[896,768]{1,0:T(8,128)(2,1)S(1)}, bf16[896,768]{1,0:T(8,128)(2,1)S(1)}, u32[]{:S(2)}, u32[]{:S(2)}) %collective-permute-start) | collective-permute-done | bytes 1376288 | tf_op jit(solution)/shard_map/ppermute | solution.py:15
  63.9 4.0 %fusion.23 = f32[896,768]{1,0:T(8,128)} fusion(f32[448,896]{1,0:T(8,128)} %get-tuple-element.14, f32[]{:T(128)S(6)} %copy.7, bf16[448,768]{1,0:T(8,128)(2,1)S(1)} %copy-done.1, f32[448]{0:T(512)S(1)} %add_rsqrt_fusion.1), kind=kOutput, calls=%fused_computation.55 | convolution fusion | flops 619200512 | bytes 5048068 | tf_op jit(solution)/shard_map/dot_general | solution.py:56
  68.0 5.2 %collective-permute-start.1 = (bf16[896,768]{1,0:T(8,128)(2,1)S(1)}, bf16[896,768]{1,0:T(8,128)(2,1)S(1)}, u32[]{:S(2)}, u32[]{:S(2)}) collective-permute-start(bf16[896,768]{1,0:T(8,128)(2,1)S(1)} %collective-permute-done), channel_id=1, source_target_pairs={{30,0},{0,2},{2,4},{4,6},{6,8},{8,10},{10,12},{12,14},{14,16},{16,... | collective-permute-start | bytes 4128776 | tf_op jit(solution)/shard_map/ppermute | solution.py:15
  73.3 15.3 %collective-permute-done.1 = bf16[896,768]{1,0:T(8,128)(2,1)S(1)} collective-permute-done((bf16[896,768]{1,0:T(8,128)(2,1)S(1)}, bf16[896,768]{1,0:T(8,128)(2,1)S(1)}, u32[]{:S(2)}, u32[]{:S(2)}) %collective-permute-start.1) | collective-permute-done | bytes 1376288 | tf_op jit(solution)/shard_map/ppermute | solution.py:15
  94.1 5.4 %collective-permute-start.2 = (bf16[896,768]{1,0:T(8,128)(2,1)S(1)}, bf16[896,768]{1,0:T(8,128)(2,1)S(1)}, u32[]{:S(2)}, u32[]{:S(2)}) collective-permute-start(bf16[896,768]{1,0:T(8,128)(2,1)S(1)} %collective-permute-done.1), channel_id=1, source_target_pairs={{30,0},{0,2},{2,4},{4,6},{6,8},{8,10},{10,12},{12,14},{14,16},{16,... | collective-permute-start | bytes 4128776 | tf_op jit(solution)/shard_map/ppermute | solution.py:15
  99.5 15.3 %collective-permute-done.2 = bf16[896,768]{1,0:T(8,128)(2,1)S(1)} collective-permute-done((bf16[896,768]{1,0:T(8,128)(2,1)S(1)}, bf16[896,768]{1,0:T(8,128)(2,1)S(1)}, u32[]{:S(2)}, u32[]{:S(2)}) %collective-permute-start.2) | collective-permute-done | bytes 1376288 | tf_op jit(solution)/shard_map/ppermute | solution.py:15
  120.3 5.2 %collective-permute-start.3 = (bf16[896,768]{1,0:T(8,128)(2,1)S(1)}, bf16[896,768]{1,0:T(8,128)(2,1)S(1)}, u32[]{:S(2)}, u32[]{:S(2)}) collective-permute-start(bf16[896,768]{1,0:T(8,128)(2,1)S(1)} %collective-permute-done.2), channel_id=1, source_target_pairs={{30,0},{0,2},{2,4},{4,6},{6,8},{8,10},{10,12},{12,14},{14,16},{16,... | collective-permute-start | bytes 4128776 | tf_op jit(solution)/shard_map/ppermute | solution.py:15
  125.6 15.3 %collective-permute-done.3 = bf16[896,768]{1,0:T(8,128)(2,1)S(1)} collective-permute-done((bf16[896,768]{1,0:T(8,128)(2,1)S(1)}, bf16[896,768]{1,0:T(8,128)(2,1)S(1)}, u32[]{:S(2)}, u32[]{:S(2)}) %collective-permute-start.3) | collective-permute-done | bytes 1376288 | tf_op jit(solution)/shard_map/ppermute | solution.py:15
  143.7 2.7 fusion.26
  147.7 5.2 %collective-permute-start.4 = (bf16[896,768]{1,0:T(8,128)(2,1)S(1)}, bf16[896,768]{1,0:T(8,128)(2,1)}, u32[]{:S(2)}, u32[]{:S(2)}) collective-permute-start(bf16[896,768]{1,0:T(8,128)(2,1)S(1)} %copy-done.13), channel_id=1, source_target_pairs={{30,0},{0,2},{2,4},{4,6},{6,8},{8,10},{10,12},{12,14},{14,16},{16,... | collective-permute-start | bytes 4128776 | tf_op jit(solution)/shard_map/ppermute | solution.py:15
  152.9 15.2 %collective-permute-done.4 = bf16[896,768]{1,0:T(8,128)(2,1)} collective-permute-done((bf16[896,768]{1,0:T(8,128)(2,1)S(1)}, bf16[896,768]{1,0:T(8,128)(2,1)}, u32[]{:S(2)}, u32[]{:S(2)}) %collective-permute-start.4) | collective-permute-done | bytes 1376288 | tf_op jit(solution)/shard_map/ppermute | solution.py:15
  168.2 4.0 %fusion.14 = (f32[448]{0:T(512)S(1)}, f32[448,896]{1,0:T(8,128)}) fusion(f32[]{:T(128)S(6)} %copy.8, bf16[896,768]{1,0:T(8,128)(2,1)} %collective-permute-done.4, bf16[448,768]{1,0:T(8,128)(2,1)S(1)} %copy-done.1, f32[448]{0:T(512)S(1)} %add_rsqrt_fusion.1, f32[]{:T(128)S(6)} %copy.7), kind=kOutput, calls=%fused_computation.26 | convolution fusion | flops 622009920 | bytes 3673608 | tf_op jit(solution)/shard_map/dot_general | solution.py:45
  172.2 10.8 %collective-permute-done.5 = f32[448,768]{1,0:T(8,128)S(1)} collective-permute-done((f32[448,768]{1,0:T(8,128)}, f32[448,768]{1,0:T(8,128)S(1)}, u32[]{:S(2)}, u32[]{:S(2)}) %collective-permute-start.5) | collective-permute-done | bytes 1376288 | tf_op jit(solution)/shard_map/ppermute | solution.py:15
  184.6 5.1 %collective-permute-start.6 = (f32[448,768]{1,0:T(8,128)S(1)}, f32[448,768]{1,0:T(8,128)S(1)}, u32[]{:S(2)}, u32[]{:S(2)}) collective-permute-start(f32[448,768]{1,0:T(8,128)S(1)} %add.176), channel_id=1, source_target_pairs={{30,0},{0,2},{2,4},{4,6},{6,8},{8,10},{10,12},{12,14},{14,16},{16,... | collective-permute-start | bytes 4128776 | tf_op jit(solution)/shard_map/ppermute | solution.py:15
  192.4 12.6 %collective-permute-done.6 = f32[448,768]{1,0:T(8,128)S(1)} collective-permute-done((f32[448,768]{1,0:T(8,128)S(1)}, f32[448,768]{1,0:T(8,128)S(1)}, u32[]{:S(2)}, u32[]{:S(2)}) %collective-permute-start.6) | collective-permute-done | bytes 1376288 | tf_op jit(solution)/shard_map/ppermute | solution.py:15
  206.5 5.2 %collective-permute-start.7 = (f32[448,768]{1,0:T(8,128)S(1)}, f32[448,768]{1,0:T(8,128)S(1)}, u32[]{:S(2)}, u32[]{:S(2)}) collective-permute-start(f32[448,768]{1,0:T(8,128)S(1)} %add.177), channel_id=1, source_target_pairs={{30,0},{0,2},{2,4},{4,6},{6,8},{8,10},{10,12},{12,14},{14,16},{16,... | collective-permute-start | bytes 4128776 | tf_op jit(solution)/shard_map/ppermute | solution.py:15
  211.7 15.2 %collective-permute-done.7 = f32[448,768]{1,0:T(8,128)S(1)} collective-permute-done((f32[448,768]{1,0:T(8,128)S(1)}, f32[448,768]{1,0:T(8,128)S(1)}, u32[]{:S(2)}, u32[]{:S(2)}) %collective-permute-start.7) | collective-permute-done | bytes 1376288 | tf_op jit(solution)/shard_map/ppermute | solution.py:15
  228.4 5.2 %collective-permute-start.8 = (f32[448,768]{1,0:T(8,128)S(1)}, f32[448,768]{1,0:T(8,128)S(1)}, u32[]{:S(2)}, u32[]{:S(2)}) collective-permute-start(f32[448,768]{1,0:T(8,128)S(1)} %add.178), channel_id=1, source_target_pairs={{30,0},{0,2},{2,4},{4,6},{6,8},{8,10},{10,12},{12,14},{14,16},{16,... | collective-permute-start | bytes 4128776 | tf_op jit(solution)/shard_map/ppermute | solution.py:15
  235.6 12.5 %reduce-scatter.15.cloned.1.call-done = f32[448,768]{1,0:T(8,128)} async-done(((f32[896,768]{1,0:T(8,128)}), f32[448,768]{1,0:T(8,128)}) %reduce-scatter.15.cloned.1.call-update) | async-done | bytes 1376272 | tf_op jit(solution)/shard_map/reduce_scatter | solution.py:59
  250.4 5.5 %collective-permute-start.9 = (f32[448,768]{1,0:T(8,128)S(1)}, f32[448,768]{1,0:T(8,128)S(1)}, u32[]{:S(2)}, u32[]{:S(2)}) collective-permute-start(f32[448,768]{1,0:T(8,128)S(1)} %add.179), channel_id=1, source_target_pairs={{30,0},{0,2},{2,4},{4,6},{6,8},{8,10},{10,12},{12,14},{14,16},{16,... | collective-permute-start | bytes 4128776 | tf_op jit(solution)/shard_map/ppermute | solution.py:15
  262.6 26.9 %reduce-scatter.17.cloned.1.call-done = f32[448,768]{1,0:T(8,128)} async-done(((f32[896,768]{1,0:T(8,128)}), f32[448,768]{1,0:T(8,128)}) %reduce-scatter.17.cloned.1.call-update) | async-done | bytes 1376272 | tf_op jit(solution)/shard_map/reduce_scatter | solution.py:59
  298.9 41.3 %collective-permute-done.10 = f32[448,768]{1,0:T(8,128)S(1)} collective-permute-done((f32[448,768]{1,0:T(8,128)S(1)}, f32[448,768]{1,0:T(8,128)S(1)}, u32[]{:S(2)}, u32[]{:S(2)}) %collective-permute-start.10) | collective-permute-done | bytes 1376288 | tf_op jit(solution)/shard_map/ppermute | solution.py:15
  (100 shorter events, 56.5 us)
Async XLA Ops:
  7.2 29.7 %all-gather.2.cloned.1.call-start = ((), (), s32[]{:S(2)}) async-start(), calls=%async_computation.6 | async-start | bytes 2064384 | tf_op jit(solution)/shard_map/all_gather | solution.py:68
  10.8 142.2 %reduce-scatter.7.cloned.1.call-start = ((), (), s32[]{:S(2)}) async-start(), calls=%async_computation.7 | async-start | bytes 4128768 | tf_op jit(solution)/shard_map/reduce_scatter | solution.py:59
  43.9 139.1 %reduce-scatter.9.cloned.1.call-start = ((), (), s32[]{:S(2)}) async-start(), calls=%async_computation.8 | async-start | bytes 4128768 | tf_op jit(solution)/shard_map/reduce_scatter | solution.py:59
  45.2 16.0 %collective-permute-start = (bf16[896,768]{1,0:T(8,128)(2,1)S(1)}, bf16[896,768]{1,0:T(8,128)(2,1)S(1)}, u32[]{:S(2)}, u32[]{:S(2)}) collective-permute-start(bf16[896,768]{1,0:T(8,128)(2,1)S(1)} %copy-done.4), channel_id=1, source_target_pairs={{30,0},{0,2},{2,4},{4,6},{6,8},{8,10},{10,12},{12,14},{14,16},{16,... | collective-permute-start | bytes 4128776 | tf_op jit(solution)/shard_map/ppermute | solution.py:15
  68.0 124.4 %reduce-scatter.11.cloned.1.call-start = ((), (), s32[]{:S(2)}) async-start(), calls=%async_computation.9 | async-start | bytes 4128768 | tf_op jit(solution)/shard_map/reduce_scatter | solution.py:59
  68.0 20.5 %collective-permute-start.1 = (bf16[896,768]{1,0:T(8,128)(2,1)S(1)}, bf16[896,768]{1,0:T(8,128)(2,1)S(1)}, u32[]{:S(2)}, u32[]{:S(2)}) collective-permute-start(bf16[896,768]{1,0:T(8,128)(2,1)S(1)} %collective-permute-done), channel_id=1, source_target_pairs={{30,0},{0,2},{2,4},{4,6},{6,8},{8,10},{10,12},{12,14},{14,16},{16,... | collective-permute-start | bytes 4128776 | tf_op jit(solution)/shard_map/ppermute | solution.py:15
  94.0 117.7 %reduce-scatter.13.cloned.1.call-start = ((), (), s32[]{:S(2)}) async-start(), calls=%async_computation.10 | async-start | bytes 4128768 | tf_op jit(solution)/shard_map/reduce_scatter | solution.py:59
  94.1 20.7 %collective-permute-start.2 = (bf16[896,768]{1,0:T(8,128)(2,1)S(1)}, bf16[896,768]{1,0:T(8,128)(2,1)S(1)}, u32[]{:S(2)}, u32[]{:S(2)}) collective-permute-start(bf16[896,768]{1,0:T(8,128)(2,1)S(1)} %collective-permute-done.1), channel_id=1, source_target_pairs={{30,0},{0,2},{2,4},{4,6},{6,8},{8,10},{10,12},{12,14},{14,16},{16,... | collective-permute-start | bytes 4128776 | tf_op jit(solution)/shard_map/ppermute | solution.py:15
  120.3 127.8 %reduce-scatter.15.cloned.1.call-start = ((), (), s32[]{:S(2)}) async-start(), calls=%async_computation.11 | async-start | bytes 4128768 | tf_op jit(solution)/shard_map/reduce_scatter | solution.py:59
  120.3 20.5 %collective-permute-start.3 = (bf16[896,768]{1,0:T(8,128)(2,1)S(1)}, bf16[896,768]{1,0:T(8,128)(2,1)S(1)}, u32[]{:S(2)}, u32[]{:S(2)}) collective-permute-start(bf16[896,768]{1,0:T(8,128)(2,1)S(1)} %collective-permute-done.2), channel_id=1, source_target_pairs={{30,0},{0,2},{2,4},{4,6},{6,8},{8,10},{10,12},{12,14},{14,16},{16,... | collective-permute-start | bytes 4128776 | tf_op jit(solution)/shard_map/ppermute | solution.py:15
  146.4 143.1 %reduce-scatter.17.cloned.1.call-start = ((), (), s32[]{:S(2)}) async-start(), calls=%async_computation.12 | async-start | bytes 4128768 | tf_op jit(solution)/shard_map/reduce_scatter | solution.py:59
  147.7 20.5 %collective-permute-start.4 = (bf16[896,768]{1,0:T(8,128)(2,1)S(1)}, bf16[896,768]{1,0:T(8,128)(2,1)}, u32[]{:S(2)}, u32[]{:S(2)}) collective-permute-start(bf16[896,768]{1,0:T(8,128)(2,1)S(1)} %copy-done.13), channel_id=1, source_target_pairs={{30,0},{0,2},{2,4},{4,6},{6,8},{8,10},{10,12},{12,14},{14,16},{16,... | collective-permute-start | bytes 4128776 | tf_op jit(solution)/shard_map/ppermute | solution.py:15
  152.9 30.1 %collective-permute-start.5 = (f32[448,768]{1,0:T(8,128)}, f32[448,768]{1,0:T(8,128)S(1)}, u32[]{:S(2)}, u32[]{:S(2)}) collective-permute-start(f32[448,768]{1,0:T(8,128)} %reduce-scatter.7.cloned.1.call-done), channel_id=1, source_target_pairs={{30,0},{0,2},{2,4},{4,6},{6,8},{8,10},{10,12},{12,14},{14,16},{16,... | collective-permute-start | bytes 4128776 | tf_op jit(solution)/shard_map/ppermute | solution.py:15
  184.6 20.4 %collective-permute-start.6 = (f32[448,768]{1,0:T(8,128)S(1)}, f32[448,768]{1,0:T(8,128)S(1)}, u32[]{:S(2)}, u32[]{:S(2)}) collective-permute-start(f32[448,768]{1,0:T(8,128)S(1)} %add.176), channel_id=1, source_target_pairs={{30,0},{0,2},{2,4},{4,6},{6,8},{8,10},{10,12},{12,14},{14,16},{16,... | collective-permute-start | bytes 4128776 | tf_op jit(solution)/shard_map/ppermute | solution.py:15
  206.5 20.5 %collective-permute-start.7 = (f32[448,768]{1,0:T(8,128)S(1)}, f32[448,768]{1,0:T(8,128)S(1)}, u32[]{:S(2)}, u32[]{:S(2)}) collective-permute-start(f32[448,768]{1,0:T(8,128)S(1)} %add.177), channel_id=1, source_target_pairs={{30,0},{0,2},{2,4},{4,6},{6,8},{8,10},{10,12},{12,14},{14,16},{16,... | collective-permute-start | bytes 4128776 | tf_op jit(solution)/shard_map/ppermute | solution.py:15
  211.7 22.0 %copy-start.3 = (bf16[448,896]{1,0:T(8,128)(2,1)S(1)}, bf16[448,896]{1,0:T(8,128)(2,1)}, u32[]{:S(2)}) copy-start(bf16[448,896]{1,0:T(8,128)(2,1)} %copy-done.2) | copy-start | bytes 2408452
  211.7 22.0 %copy-start.5 = (bf16[896,768]{1,0:T(8,128)(2,1)S(1)}, bf16[896,768]{1,0:T(8,128)(2,1)}, u32[]{:S(2)}) copy-start(bf16[896,768]{1,0:T(8,128)(2,1)} %all-gather.2.cloned.1.call-done) | copy-start | bytes 4128772
  228.4 20.5 %collective-permute-start.8 = (f32[448,768]{1,0:T(8,128)S(1)}, f32[448,768]{1,0:T(8,128)S(1)}, u32[]{:S(2)}, u32[]{:S(2)}) collective-permute-start(f32[448,768]{1,0:T(8,128)S(1)} %add.178), channel_id=1, source_target_pairs={{30,0},{0,2},{2,4},{4,6},{6,8},{8,10},{10,12},{12,14},{14,16},{16,... | collective-permute-start | bytes 4128776 | tf_op jit(solution)/shard_map/ppermute | solution.py:15
  248.1 7.8 %copy-start.15 = (f32[448,768]{1,0:T(8,128)S(1)}, f32[448,768]{1,0:T(8,128)}, u32[]{:S(2)}) copy-start(f32[448,768]{1,0:T(8,128)} %fusion.41) | copy-start | bytes 4128772
  250.4 8.2 %copy-start.9 = (bf16[896,768]{1,0:T(8,128)(2,1)S(1)}, bf16[896,768]{1,0:T(8,128)(2,1)}, u32[]{:S(2)}) copy-start(bf16[896,768]{1,0:T(8,128)(2,1)} %copy-done.8) | copy-start | bytes 4128772
  250.4 8.2 %copy-start.17 = (f32[448,896]{1,0:T(8,128)S(1)}, f32[448,896]{1,0:T(8,128)}, u32[]{:S(2)}) copy-start(f32[448,896]{1,0:T(8,128)} %copy-done.16) | copy-start | bytes 4816900
  250.4 39.0 %collective-permute-start.9 = (f32[448,768]{1,0:T(8,128)S(1)}, f32[448,768]{1,0:T(8,128)S(1)}, u32[]{:S(2)}, u32[]{:S(2)}) collective-permute-start(f32[448,768]{1,0:T(8,128)S(1)} %add.179), channel_id=1, source_target_pairs={{30,0},{0,2},{2,4},{4,6},{6,8},{8,10},{10,12},{12,14},{14,16},{16,... | collective-permute-start | bytes 4128776 | tf_op jit(solution)/shard_map/ppermute | solution.py:15
  291.1 49.1 %collective-permute-start.10 = (f32[448,768]{1,0:T(8,128)S(1)}, f32[448,768]{1,0:T(8,128)S(1)}, u32[]{:S(2)}, u32[]{:S(2)}) collective-permute-start(f32[448,768]{1,0:T(8,128)S(1)} %add.180), channel_id=1, source_target_pairs={{10,0},{12,2},{14,4},{16,6},{18,8},{20,10},{22,12},{24,14},{26,16}... | collective-permute-start | bytes 4128776 | tf_op jit(solution)/shard_map/ppermute | solution.py:15
  297.5 42.7 %copy-start = (bf16[448,768]{1,0:T(8,128)(2,1)S(1)}, bf16[448,768]{1,0:T(8,128)(2,1)}, u32[]{:S(2)}) copy-start(bf16[448,768]{1,0:T(8,128)(2,1)} %param.5) | copy-start | bytes 2064388
  (18 other events, 58.3 us)
Sparse Core Ops, SparseCore 0:
  10.9 25.9 all-gather.1
  44.1 39.0 reduce-scatter.6
  85.4 38.9 reduce-scatter.8
  126.6 39.0 reduce-scatter.10
  167.9 38.9 reduce-scatter.12
  209.0 39.0 reduce-scatter.14
  250.4 38.9 reduce-scatter.16
where the time goes:
time: 349 us
  waiting for transfers between devices  221 us (63%)
  matrix products  45.1 us (13%)
  starting transfers between devices  44.1 us (13%)
  between operations  15.6 us (4%)
  other arithmetic  15.1 us (4%)
  local copies, waits for them, and re-layouts  7.78 us (2%)
    ppermute x11, waiting for transfers between devices, passed_along(): return lax.ppermute(block, axis, route)  157 us
    ppermute x11, starting transfers between devices, passed_along(): return lax.ppermute(block, axis, route)  43.8 us
    reduce_scatter x6, waiting for transfers between devices, visit(): lax.psum_scatter(text_grad, 'pair', scatter_dimension=0, tiled=True)  39.4 us
    all_gather x1, waiting for transfers between devices, body(): text_now = lax.all_gather(text_emb, 'pair', axis=0, tiled=True)  24.5 us
    dot_general x6, matrix products, visit(): lax.dot_general(weights_bf, image_emb, (((0,), (0,)), ((), ())), preferre...  17.1 us
    dot_general x6, matrix products, visit(): lax.dot_general(image_emb, text_now, (((1,), (1,)), ((), ())), preferred_...  15.3 us
    dot_general x6, matrix products, visit(): jnp.dot(weights_bf, text_now, preferred_element_type=jnp.float32)  12.7 us
    unnamed x48, local copies, waits for them, and re-layouts  7.78 us
  transfers between devices with their start and end apart: 18, of which 13 were waited for; matrix products, arithmetic and copies ran while one was open for 14% of the time, Pallas kernels for 0%

commit v1 on v0

v1 whole, which is shorter than its diff:
```python
import functools

import jax
import jax.numpy as jnp
from jax import lax
from jax.experimental import pallas as pl
from jax.experimental.pallas import tpu as pltpu
from jax.sharding import PartitionSpec as P

STEPS = 6
EPSILON = 1e-06
MESH = pl.DeviceIdType.MESH

OWN, FAR, NEAR, FAR_SIB, NEAR_SIB, LAST = range(6)
S_FAR, S_NEAR, S_OWN_SIB, S_FAR_SIB, S_NEAR_SIB, S_LAST = range(6)


def unit_rows(features):
    widened = features.astype(jnp.float32)
    inverse = lax.rsqrt(jnp.sum(widened * widened, axis=1, keepdims=True) + EPSILON)
    return (widened * inverse, inverse)


def tangent(unit, inverse, direction):
    return inverse * (direction - unit * jnp.sum(unit * direction, axis=1, keepdims=True))


def kernel(
    n_blk,
    images_ref,
    texts_ref,
    scale_ref,
    bias_ref,
    loss_out,
    grad_images,
    grad_texts,
    keys,
    part,
    acc,
    out_part,
    in_part,
    loss_acc,
    loss_send,
    loss_recv,
    send_sem,
    recv_sem,
    part_sem,
    sum_sem,
    loss_sem,
):
    rows, width = images_ref.shape
    chunk = rows // 2
    me = lax.axis_index("blk")
    pair = lax.axis_index("pair")
    other = 1 - pair
    xpartner = jnp.where(lax.rem(me // 2, 2) == 0, me + 2, me - 2)

    def wrap(position):
        return lax.rem(position + n_blk, n_blk)

    barrier = pltpu.get_barrier_semaphore()
    peers = [(wrap(me + d), pair) for d in (-4, -3, -1, 1, 3, 4)]
    peers += [(xpartner, pair), (me, other)]
    for peer in peers:
        pl.semaphore_signal(barrier, inc=1, device_id=peer, device_id_type=MESH)

    scale = scale_ref[0]
    bias = bias_ref[0]

    text_unit, _ = unit_rows(texts_ref[...])
    keys[0, OWN] = text_unit.astype(jnp.bfloat16)
    image_unit, _ = unit_rows(images_ref[...])
    keys[1, OWN] = image_unit.astype(jnp.bfloat16)
    pl.semaphore_wait(barrier, len(peers))

    def place(side):
        return me if side == 0 else n_blk - 1 - me

    def device(side, position):
        position = wrap(position)
        return (position if side == 0 else n_blk - 1 - position, pair)

    def block_copy(side, send, source, target, c, dst):
        span = pl.ds(c * chunk, chunk)
        return pltpu.make_async_remote_copy(
            src_ref=keys.at[side, source, span],
            dst_ref=keys.at[side, target, span],
            send_sem=send_sem.at[side, send, c],
            recv_sem=recv_sem.at[side, target, c],
            device_id=dst,
            device_id_type=MESH,
        )

    def far(side, c):
        return block_copy(side, S_FAR, OWN, FAR, c, device(side, place(side) + 4))

    def near(side, c, source):
        return block_copy(side, S_NEAR, source, NEAR, c, (xpartner, pair))

    def own_sib(side, c):
        return block_copy(side, S_OWN_SIB, OWN, LAST, c, device(side, place(side) + 1))

    def sib(side, send, source, target, c):
        position = place(side)
        core = lax.rem(position, 2)
        return block_copy(side, send, source, target, c, device(side, position + 1 - 2 * core))

    def last(side, c, source):
        step = 1 if source == FAR else 3
        send = S_LAST if source == FAR else S_OWN_SIB
        return block_copy(side, send, source, LAST, c, device(side, place(side) + step))

    def roles(side):
        position = place(side)
        even_chip = lax.rem(position // 2, 2) == 0
        first_core = lax.rem(position, 2) == 0
        return even_chip, first_core

    part_copies = []
    for side in (0, 1):
        part_copies.append(
            pltpu.make_async_remote_copy(
                src_ref=keys.at[1 - side, OWN],
                dst_ref=part.at[side],
                send_sem=part_sem.at[0, side],
                recv_sem=part_sem.at[1, side],
                device_id=(me, other),
                device_id_type=MESH,
            )
        )

    for side in (0, 1):
        even_chip, first_core = roles(side)
        for c in (0, 1):
            far(side, c).start()

            @pl.when(even_chip)
            def _():
                near(side, c, OWN).start()

        part_copies[side].start()

        @pl.when(first_core)
        def _():
            for c in (0, 1):
                own_sib(side, c).start()

    def after_far(side):
        even_chip, first_core = roles(side)
        for c in (0, 1):
            far(side, c).wait_recv()

            @pl.when(jnp.logical_not(even_chip))
            def _():
                near(side, c, FAR).start()

            @pl.when(jnp.logical_and(even_chip, jnp.logical_not(first_core)))
            def _():
                last(side, c, FAR).start()

            sib(side, S_FAR_SIB, FAR, FAR_SIB, c).start()

    def after_near(side):
        even_chip, first_core = roles(side)
        for c in (0, 1):
            near(side, c, OWN).wait_recv()

            @pl.when(jnp.logical_and(even_chip, jnp.logical_not(first_core)))
            def _():
                last(side, c, NEAR).start()

            sib(side, S_NEAR_SIB, NEAR, NEAR_SIB, c).start()

    def wait_block(side, slot):
        for c in (0, 1):
            own_like = block_copy(side, S_FAR, OWN, slot, c, (me, other))
            own_like.wait_recv()

    acc[...] = jnp.zeros_like(acc)
    loss_acc[...] = jnp.zeros_like(loss_acc)

    def tile(side, half, slot, diagonal):
        query = keys.at[1 - side, OWN] if half == 0 else part.at[side]
        key = keys[side, slot]
        for c in range(2):
            span = pl.ds(c * chunk, chunk)
            dots = lax.dot_general(
                query[span, :], key, (((1,), (1,)), ((), ())), preferred_element_type=jnp.float32
            )
            value = scale * dots + bias
            if diagonal:
                row = lax.broadcasted_iota(jnp.int32, dots.shape, 0) + c * chunk
                column = lax.broadcasted_iota(jnp.int32, dots.shape, 1)
                sign = jnp.where(row == column, -1.0, 1.0)
                value = sign * value
                gain = sign * scale
            else:
                gain = scale
            grown = jnp.exp(value)
            total = 1.0 + grown
            weights = (gain * (grown / total)).astype(jnp.bfloat16)
            acc[side, half, span, :] += jnp.dot(weights, key, preferred_element_type=jnp.float32)
            if side == 0:
                loss = jnp.where(grown < 2.0**-11, grown, jnp.log(total))
                loss_acc[half, span, :] += jnp.broadcast_to(
                    jnp.sum(loss, axis=1, keepdims=True), (chunk, 128)
                )

    sum_copies = []
    for side in (0, 1):
        sum_copies.append(
            pltpu.make_async_remote_copy(
                src_ref=out_part.at[side],
                dst_ref=in_part.at[side],
                send_sem=sum_sem.at[0, side],
                recv_sem=sum_sem.at[1, side],
                device_id=(me, other),
                device_id_type=MESH,
            )
        )
    loss_copy = pltpu.make_async_remote_copy(
        src_ref=loss_send,
        dst_ref=loss_recv,
        send_sem=loss_sem.at[0],
        recv_sem=loss_sem.at[1],
        device_id=(me, other),
        device_id_type=MESH,
    )

    def send_part(side):
        out_part[side] = acc[side, 1].astype(jnp.bfloat16)
        sum_copies[side].start()

    tile(0, 0, OWN, True)
    tile(1, 0, OWN, True)
    after_far(0)
    tile(0, 0, FAR, False)
    after_far(1)
    tile(1, 0, FAR, False)
    part_copies[0].wait_recv()
    after_near(0)

    def both(side, slot):
        tile(side, 1, slot, False)
        tile(side, 0, slot, False)

    tile(0, 1, OWN, False)
    tile(0, 1, FAR, False)
    after_near(1)
    part_copies[1].wait_recv()
    both(0, NEAR)
    tile(1, 1, OWN, False)
    tile(1, 1, FAR, False)
    both(1, NEAR)

    def rest(side):
        @pl.loop(FAR_SIB, LAST + 1)
        def _(slot):
            wait_block(side, slot)
            tile(side, 1, slot, False)

        send_part(side)
        if side == 0:
            loss_send[...] = jnp.transpose(loss_acc[1])[:8, :]
            loss_copy.start()

        @pl.loop(FAR_SIB, LAST + 1)
        def _(slot):
            tile(side, 0, slot, False)

    rest(0)
    rest(1)

    def finish(side, features, out):
        sum_copies[side].wait_recv()
        for c in range(2):
            span = pl.ds(c * chunk, chunk)
            unit, inverse = unit_rows(features[span, :])
            direction = acc[side, 0, span, :] + in_part[side, span, :].astype(jnp.float32)
            out[span, :] = tangent(unit, inverse, direction)

    finish(0, images_ref, grad_images)
    loss_copy.wait_recv()
    window = STEPS * 2 * rows
    loss_out[...] = (jnp.transpose(loss_acc[0])[:8, :] + loss_recv[...]) / window
    finish(1, texts_ref, grad_texts)

    for side in (0, 1):
        even_chip, first_core = roles(side)
        part_copies[side].wait_send()
        sum_copies[side].wait_send()
        for c in (0, 1):
            far(side, c).wait_send()
            near(side, c, OWN).wait_send()
            sib(side, S_FAR_SIB, FAR, FAR_SIB, c).wait_send()
            sib(side, S_NEAR_SIB, NEAR, NEAR_SIB, c).wait_send()

            @pl.when(first_core)
            def _():
                own_sib(side, c).wait_send()

            @pl.when(jnp.logical_and(even_chip, jnp.logical_not(first_core)))
            def _():
                last(side, c, FAR).wait_send()
                last(side, c, NEAR).wait_send()

    loss_copy.wait_send()


def body(n_blk, images, texts, scale, bias):
    rows, width = images.shape
    vmem = pl.BlockSpec(memory_space=pltpu.VMEM)
    smem = pl.BlockSpec(memory_space=pltpu.SMEM)
    loss, grad_images, grad_texts = pl.pallas_call(
        functools.partial(kernel, n_blk),
        out_shape=(
            jax.ShapeDtypeStruct((8, rows), jnp.float32),
            jax.ShapeDtypeStruct((rows, width), jnp.float32),
            jax.ShapeDtypeStruct((rows, width), jnp.float32),
        ),
        in_specs=[vmem, vmem, smem, smem],
        out_specs=(vmem, vmem, vmem),
        scratch_shapes=[
            pltpu.VMEM((2, STEPS, rows, width), jnp.bfloat16),
            pltpu.VMEM((2, rows, width), jnp.bfloat16),
            pltpu.VMEM((2, 2, rows, width), jnp.float32),
            pltpu.VMEM((2, rows, width), jnp.bfloat16),
            pltpu.VMEM((2, rows, width), jnp.bfloat16),
            pltpu.VMEM((2, rows, 128), jnp.float32),
            pltpu.VMEM((8, rows), jnp.float32),
            pltpu.VMEM((8, rows), jnp.float32),
            pltpu.SemaphoreType.DMA((2, 6, 2)),
            pltpu.SemaphoreType.DMA((2, 6, 2)),
            pltpu.SemaphoreType.DMA((2, 2)),
            pltpu.SemaphoreType.DMA((2, 2)),
            pltpu.SemaphoreType.DMA((2,)),
        ],
        compiler_params=pltpu.CompilerParams(
            collective_id=0, has_side_effects=True, vmem_limit_bytes=56 * 1024 * 1024
        ),
    )(images, texts, scale.reshape(1), bias.reshape(1))
    return (loss[0], grad_images, grad_texts)


def solution(mesh):
    in_specs = (P(("blk", "pair"), None), P(("blk", "pair"), None), P(), P())
    out_specs = (P(("blk", "pair")), P(("blk", "pair"), None), P(("blk", "pair"), None))
    return jax.shard_map(
        functools.partial(body, mesh.shape["blk"]),
        mesh=mesh,
        in_specs=in_specs,
        out_specs=out_specs,
        check_vma=False,
    )
```

time: 349 us -> 97.1 us (0.28)
  waiting for transfers between devices: 221 us -> 0 us
  Pallas kernels: 0 us -> 89.1 us
  matrix products: 45.1 us -> 0 us
  starting transfers between devices: 44.1 us -> 0 us
  other arithmetic: 15.1 us -> 0 us
  between operations: 15.6 us -> 1.93 us
    ppermute x11 -> x0, waiting for transfers between devices: 157 us -> none  [passed_along(): return lax.ppermute(block, axis, route)]
    pallas_call x0 -> x1, Pallas kernels: none -> 89.1 us  [body(): pl.pallas_call(functools.partial(kernel, n_blk), out_shape=(jax.ShapeDtyp...]
    dot_general x18 -> x0, matrix products: 45.1 us -> none  [the longest x6 17.1 us: visit(): lax.dot_general(weights_bf, image_emb, (((0,), (0,)), ((), ())), preferre...]
    ppermute x11 -> x0, starting transfers between devices: 43.8 us -> none  [passed_along(): return lax.ppermute(block, axis, route)]
    reduce_scatter x6 -> x0, waiting for transfers between devices: 39.4 us -> none  [visit(): lax.psum_scatter(text_grad, 'pair', scatter_dimension=0, tiled=True)]
    all_gather x1 -> x0, waiting for transfers between devices: 24.5 us -> none  [body(): text_now = lax.all_gather(text_emb, 'pair', axis=0, tiled=True)]
    add x6 -> x0, other arithmetic: 7.64 us -> none  [the longest x5 7.64 us: body(): partial_value = text_grad if offset == 0 else partial_value + text_grad]
    unnamed x48 -> x4, local copies, waits for them, and re-layouts: 7.78 us -> 3.69 us
  transfers between devices with their start and end apart: 18 -> 0, of which waited for: 13 -> 0; matrix products, arithmetic and copies ran while one was open for 14% -> 0% of each run, Pallas kernels for 0% -> 0%
where the time goes in v1:
time: 97.1 us; the launch traced here: 96 us
  Pallas kernels  89.1 us (92%)
  local copies, waits for them, and re-layouts  4.99 us (5%)
  between operations  1.93 us (2%)
    pallas_call x1, Pallas kernels, body(): pl.pallas_call(functools.partial(kernel, n_blk), out_shape=(jax.ShapeDtyp...  89.1 us
    unnamed x4, local copies, waits for them, and re-layouts  3.69 us

profile of v1, /device:TPU:27, one launch (start us, length us, event | category | flops | bytes accessed | tf_op | source)
XLA Modules:
  0.0 96.0 jit_solution(10010344728599960891)
XLA Ops:
  1.9 89.1 %shard_map.67 = (f32[8,448]{1,0:T(8,128)}, f32[448,768]{1,0:T(8,128)}, f32[448,768]{1,0:T(8,128)}) custom-call(bf16[448,768]{1,0:T(8,128)(2,1)} %images_ref.1, bf16[448,768]{1,0:T(8,128)(2,1)} %texts_ref.1, f32[1]{0:T(128)} %bitcast.3.scale_ref, f32[1]{0:T(128)} %bitcast.4.bias_ref), custom_call_target="tpu_custom_call" | custom-call | tf_op jit(solution)/shard_map/pallas_call | solution.py:314
  91.0 1.3 %slice.3 = f32[1,448]{1,0:T(1,128)} slice(f32[8,448]{1,0:T(8,128)} %get-tuple-element.6), slice={[0:1], [0:448]} | slice | bytes 3584 | tf_op jit(solution)/shard_map/slice | solution.py:342
  92.3 0.0 copy-start
  92.3 2.6 %copy.11 = f32[448,768]{1,0:T(8,128)} copy(f32[448,768]{1,0:T(8,128)} %get-tuple-element.13) | data formatting | bytes 2752512
  94.9 0.0 copy-done
  94.9 1.1 %copy.12 = f32[448,768]{1,0:T(8,128)} copy(f32[448,768]{1,0:T(8,128)S(1)} %copy-done) | data formatting | bytes 2752512
Async XLA Ops:
  92.3 2.6 %copy-start = (f32[448,768]{1,0:T(8,128)S(1)}, f32[448,768]{1,0:T(8,128)}, u32[]{:S(2)}) copy-start(f32[448,768]{1,0:T(8,128)} %get-tuple-element.14) | copy-start | bytes 4128772

commit v2 on v0

v2 whole, which is shorter than its diff:
```python
import functools

import jax
import jax.numpy as jnp
from jax import lax
from jax.experimental import pallas as pl
from jax.experimental.pallas import tpu as pltpu
from jax.sharding import PartitionSpec as P

STEPS = 6
EPSILON = 1e-06
MESH = pl.DeviceIdType.MESH

OWN, FAR, NEAR, FAR_SIB, NEAR_SIB, LAST = range(6)
S_FAR, S_NEAR, S_OWN_SIB, S_FAR_SIB, S_NEAR_SIB, S_LAST = range(6)


def unit_rows(features):
    widened = features.astype(jnp.float32)
    inverse = lax.rsqrt(jnp.sum(widened * widened, axis=1, keepdims=True) + EPSILON)
    return (widened * inverse, inverse)


def tangent(unit, inverse, direction):
    return inverse * (direction - unit * jnp.sum(unit * direction, axis=1, keepdims=True))


R_FAR, R_NEAR, R_OWN, R_LAST_FAR, R_LAST_NEAR, R_X, R_DONE = range(7)
O_FAR_SIB, O_NEAR_SIB, O_LAST, O_NEAR, O_FAR = range(5)


def kernel(
    n_blk,
    images_ref,
    texts_ref,
    scale_ref,
    bias_ref,
    loss_out,
    grad_images,
    grad_texts,
    keys,
    query_own,
    query_other,
    acc,
    text_acc,
    leave,
    back,
    out_part,
    in_part,
    loss_acc,
    loss_send,
    loss_recv,
    send_sem,
    recv_sem,
    leave_sem,
    back_sem,
    part_sem,
    sum_sem,
    loss_sem,
):
    rows, width = images_ref.shape
    chunk = rows // 2
    me = lax.axis_index("blk")
    pair = lax.axis_index("pair")
    other = 1 - pair
    even_chip = lax.rem(me // 2, 2) == 0
    odd_chip = jnp.logical_not(even_chip)
    first_core = lax.rem(me, 2) == 0
    second_core = jnp.logical_not(first_core)
    relay = jnp.logical_and(even_chip, second_core)
    xpartner = (jnp.where(even_chip, me + 2, me - 2), pair)
    sibling = (me + 1 - 2 * lax.rem(me, 2), pair)

    def at(distance):
        return (lax.rem(me + distance + n_blk, n_blk), pair)

    barrier = pltpu.get_barrier_semaphore()
    peers = [at(d) for d in (-4, -3, -1, 1, 3, 4)] + [xpartner, (me, other)]
    for peer in peers:
        pl.semaphore_signal(barrier, inc=1, device_id=peer, device_id_type=MESH)

    scale = scale_ref[0]
    bias = bias_ref[0]
    keys[OWN] = unit_rows(texts_ref[...])[0].astype(jnp.bfloat16)
    query_own[...] = unit_rows(images_ref[...])[0].astype(jnp.bfloat16)
    pl.semaphore_wait(barrier, len(peers))

    def key_copy(send, source, target, c, dst):
        span = pl.ds(c * chunk, chunk)
        return pltpu.make_async_remote_copy(
            src_ref=keys.at[source, span],
            dst_ref=keys.at[target, span],
            send_sem=send_sem.at[send, c],
            recv_sem=recv_sem.at[target, c],
            device_id=dst,
            device_id_type=MESH,
        )

    def far(c):
        return key_copy(S_FAR, OWN, FAR, c, at(4))

    def near(c, source):
        return key_copy(S_NEAR, source, NEAR, c, xpartner)

    def own_sib(c):
        return key_copy(S_OWN_SIB, OWN, LAST, c, sibling)

    def far_sib(c):
        return key_copy(S_FAR_SIB, FAR, FAR_SIB, c, sibling)

    def near_sib(c):
        return key_copy(S_NEAR_SIB, NEAR, NEAR_SIB, c, sibling)

    def last_far(c):
        return key_copy(S_LAST, FAR, LAST, c, at(1))

    def last_near(c):
        return key_copy(S_OWN_SIB, NEAR, LAST, c, at(3))

    def sum_copy(source, target, c, dst):
        span = pl.ds(c * chunk, chunk)
        return pltpu.make_async_remote_copy(
            src_ref=leave.at[source, span],
            dst_ref=back.at[target, span],
            send_sem=leave_sem.at[source, c],
            recv_sem=back_sem.at[target, c],
            device_id=dst,
            device_id_type=MESH,
        )

    part_copy = pltpu.make_async_remote_copy(
        src_ref=query_own,
        dst_ref=query_other,
        send_sem=part_sem.at[0],
        recv_sem=part_sem.at[1],
        device_id=(me, other),
        device_id_type=MESH,
    )
    part_sum = pltpu.make_async_remote_copy(
        src_ref=out_part,
        dst_ref=in_part,
        send_sem=sum_sem.at[0],
        recv_sem=sum_sem.at[1],
        device_id=(me, other),
        device_id_type=MESH,
    )
    loss_copy = pltpu.make_async_remote_copy(
        src_ref=loss_send,
        dst_ref=loss_recv,
        send_sem=loss_sem.at[0],
        recv_sem=loss_sem.at[1],
        device_id=(me, other),
        device_id_type=MESH,
    )

    part_copy.start()
    for c in (0, 1):
        far(c).start()

        @pl.when(even_chip)
        def _():
            near(c, OWN).start()

    @pl.when(first_core)
    def _():
        for c in (0, 1):
            own_sib(c).start()

    def after_far(c):
        far(c).wait_recv()

        @pl.when(odd_chip)
        def _():
            near(c, FAR).start()

        @pl.when(relay)
        def _():
            last_far(c).start()

        far_sib(c).start()

    def after_near(c):
        near(c, OWN).wait_recv()

        @pl.when(relay)
        def _():
            last_near(c).start()

        near_sib(c).start()

    acc[...] = jnp.zeros_like(acc)
    loss_acc[...] = jnp.zeros_like(loss_acc)

    def tile(half, slot, diagonal=False, fresh=False):
        query = query_own if half == 0 else query_other
        key = keys[slot]
        pieces = []
        for c in range(2):
            span = pl.ds(c * chunk, chunk)
            dots = lax.dot_general(
                query[span, :], key, (((1,), (1,)), ((), ())), preferred_element_type=jnp.float32
            )
            value = scale * dots + bias
            gain = scale
            if diagonal:
                row = lax.broadcasted_iota(jnp.int32, dots.shape, 0) + c * chunk
                column = lax.broadcasted_iota(jnp.int32, dots.shape, 1)
                sign = jnp.where(row == column, -1.0, 1.0)
                value = sign * value
                gain = sign * scale
            grown = jnp.exp(value)
            total = 1.0 + grown
            weights = (gain * (grown / total)).astype(jnp.bfloat16)
            pieces.append(weights)
            acc[half, span, :] += jnp.dot(weights, key, preferred_element_type=jnp.float32)
            loss = jnp.where(grown < 2.0**-11, grown, jnp.log(total))
            loss_acc[half, span, :] += jnp.broadcast_to(
                jnp.sum(loss, axis=1, keepdims=True), (chunk, 128)
            )
        text_term = lax.dot_general(
            jnp.concatenate(pieces, axis=0),
            query[...],
            (((0,), (0,)), ((), ())),
            preferred_element_type=jnp.float32,
        )
        if fresh:
            text_acc[slot] = text_term
        else:
            text_acc[slot] += text_term

    def both(slot):
        tile(1, slot, fresh=True)
        tile(0, slot)

    def depart(slot, source, c):
        span = pl.ds(c * chunk, chunk)
        leave[source, span, :] = text_acc[slot, span, :].astype(jnp.bfloat16)

    def term(target, c):
        return back[target, pl.ds(c * chunk, chunk), :].astype(jnp.float32)

    tile(0, OWN, diagonal=True, fresh=True)
    after_far(0)
    after_far(1)
    tile(0, FAR, fresh=True)
    part_copy.wait_recv()
    tile(1, OWN)
    after_near(0)
    after_near(1)
    tile(1, FAR)

    def wait_keys(slot):
        for c in (0, 1):
            key_copy(S_FAR, OWN, slot, c, sibling).wait_recv()

    wait_keys(FAR_SIB)
    both(FAR_SIB)
    for c in (0, 1):
        depart(FAR_SIB, O_FAR_SIB, c)
        sum_copy(O_FAR_SIB, R_FAR, c, sibling).start()
    wait_keys(NEAR_SIB)
    both(NEAR_SIB)
    for c in (0, 1):
        depart(NEAR_SIB, O_NEAR_SIB, c)
        sum_copy(O_NEAR_SIB, R_NEAR, c, sibling).start()
    both(NEAR)

    def pass_on(slot, source, target, dst, arrivals, c):
        span = pl.ds(c * chunk, chunk)
        total = text_acc[slot, span, :]
        for arrival in arrivals:
            sum_copy(source, arrival, c, sibling).wait_recv()
            total += term(arrival, c)
        leave[source, span, :] = total.astype(jnp.bfloat16)
        sum_copy(source, target, c, dst).start()

    def send_near(c, arrivals):
        pass_on(NEAR, O_NEAR, R_X, xpartner, arrivals, c)

    def send_far(c, arrivals):
        pass_on(FAR, O_FAR, R_DONE, at(-4), arrivals, c)

    free = jnp.logical_not(relay)
    early = jnp.logical_and(even_chip, first_core)

    @pl.when(free)
    def _():
        for c in (0, 1):
            send_near(c, (R_NEAR,))

    @pl.when(early)
    def _():
        for c in (0, 1):
            send_far(c, (R_FAR,))

    wait_keys(LAST)
    both(LAST)
    for c in (0, 1):
        depart(LAST, O_LAST, c)

        @pl.when(second_core)
        def _():
            sum_copy(O_LAST, R_OWN, c, sibling).start()

        @pl.when(jnp.logical_and(first_core, odd_chip))
        def _():
            sum_copy(O_LAST, R_LAST_FAR, c, at(-1)).start()

        @pl.when(early)
        def _():
            sum_copy(O_LAST, R_LAST_NEAR, c, at(-3)).start()

    out_part[...] = acc[1].astype(jnp.bfloat16)
    part_sum.start()
    loss_send[...] = jnp.transpose(loss_acc[1])[:8, :]
    loss_copy.start()

    for c in (0, 1):

        @pl.when(relay)
        def _():
            send_near(c, (R_NEAR, R_LAST_NEAR))

    for c in (0, 1):

        @pl.when(odd_chip)
        def _():
            send_far(c, (R_FAR, R_X))

        @pl.when(relay)
        def _():
            send_far(c, (R_FAR, R_LAST_FAR))

    part_sum.wait_recv()
    for c in (0, 1):
        span = pl.ds(c * chunk, chunk)
        unit, inverse = unit_rows(images_ref[span, :])
        direction = acc[0, span, :] + in_part[span, :].astype(jnp.float32)
        grad_images[span, :] = tangent(unit, inverse, direction)
    loss_copy.wait_recv()
    window = STEPS * 2 * rows
    loss_out[...] = (jnp.transpose(loss_acc[0])[:8, :] + loss_recv[...]) / window

    for c in (0, 1):
        span = pl.ds(c * chunk, chunk)

        @pl.when(first_core)
        def _():
            sum_copy(O_LAST, R_OWN, c, sibling).wait_recv()
            text_acc[OWN, span, :] += term(R_OWN, c)

        @pl.when(even_chip)
        def _():
            sum_copy(O_NEAR, R_X, c, xpartner).wait_recv()
            text_acc[OWN, span, :] += term(R_X, c)

        sum_copy(O_FAR, R_DONE, c, at(-4)).wait_recv()
        unit, inverse = unit_rows(texts_ref[span, :])
        direction = text_acc[OWN, span, :] + term(R_DONE, c)
        grad_texts[span, :] = tangent(unit, inverse, direction)

    part_copy.wait_send()
    part_sum.wait_send()
    loss_copy.wait_send()
    for c in (0, 1):
        far(c).wait_send()
        near(c, OWN).wait_send()
        far_sib(c).wait_send()
        near_sib(c).wait_send()
        for source in (O_FAR_SIB, O_NEAR_SIB, O_LAST, O_NEAR, O_FAR):
            sum_copy(source, R_FAR, c, sibling).wait_send()

        @pl.when(first_core)
        def _():
            own_sib(c).wait_send()

        @pl.when(relay)
        def _():
            last_far(c).wait_send()
            last_near(c).wait_send()


def body(n_blk, images, texts, scale, bias):
    rows, width = images.shape
    vmem = pl.BlockSpec(memory_space=pltpu.VMEM)
    smem = pl.BlockSpec(memory_space=pltpu.SMEM)
    loss, grad_images, grad_texts = pl.pallas_call(
        functools.partial(kernel, n_blk),
        out_shape=(
            jax.ShapeDtypeStruct((8, rows), jnp.float32),
            jax.ShapeDtypeStruct((rows, width), jnp.float32),
            jax.ShapeDtypeStruct((rows, width), jnp.float32),
        ),
        in_specs=[vmem, vmem, smem, smem],
        out_specs=(vmem, vmem, vmem),
        scratch_shapes=[
            pltpu.VMEM((STEPS, rows, width), jnp.bfloat16),
            pltpu.VMEM((rows, width), jnp.bfloat16),
            pltpu.VMEM((rows, width), jnp.bfloat16),
            pltpu.VMEM((2, rows, width), jnp.float32),
            pltpu.VMEM((STEPS, rows, width), jnp.float32),
            pltpu.VMEM((5, rows, width), jnp.bfloat16),
            pltpu.VMEM((7, rows, width), jnp.bfloat16),
            pltpu.VMEM((rows, width), jnp.bfloat16),
            pltpu.VMEM((rows, width), jnp.bfloat16),
            pltpu.VMEM((2, rows, 128), jnp.float32),
            pltpu.VMEM((8, rows), jnp.float32),
            pltpu.VMEM((8, rows), jnp.float32),
            pltpu.SemaphoreType.DMA((6, 2)),
            pltpu.SemaphoreType.DMA((6, 2)),
            pltpu.SemaphoreType.DMA((5, 2)),
            pltpu.SemaphoreType.DMA((7, 2)),
            pltpu.SemaphoreType.DMA((2,)),
            pltpu.SemaphoreType.DMA((2,)),
            pltpu.SemaphoreType.DMA((2,)),
        ],
        compiler_params=pltpu.CompilerParams(
            collective_id=0, has_side_effects=True, vmem_limit_bytes=56 * 1024 * 1024
        ),
    )(images, texts, scale.reshape(1), bias.reshape(1))
    return (loss[0], grad_images, grad_texts)


def solution(mesh):
    in_specs = (P(("blk", "pair"), None), P(("blk", "pair"), None), P(), P())
    out_specs = (P(("blk", "pair")), P(("blk", "pair"), None), P(("blk", "pair"), None))
    return jax.shard_map(
        functools.partial(body, mesh.shape["blk"]),
        mesh=mesh,
        in_specs=in_specs,
        out_specs=out_specs,
        check_vma=False,
    )
```

time: 349 us -> 79.7 us (0.23)
  waiting for transfers between devices: 221 us -> 0 us
  Pallas kernels: 0 us -> 71.6 us
  matrix products: 45.1 us -> 0 us
  starting transfers between devices: 44.1 us -> 0 us
  other arithmetic: 15.1 us -> 0 us
  between operations: 15.6 us -> 1.93 us
    ppermute x11 -> x0, waiting for transfers between devices: 157 us -> none  [passed_along(): return lax.ppermute(block, axis, route)]
    pallas_call x0 -> x1, Pallas kernels: none -> 71.6 us  [body(): pl.pallas_call(functools.partial(kernel, n_blk), out_shape=(jax.ShapeDtyp...]
    dot_general x18 -> x0, matrix products: 45.1 us -> none  [the longest x6 17.1 us: visit(): lax.dot_general(weights_bf, image_emb, (((0,), (0,)), ((), ())), preferre...]
    ppermute x11 -> x0, starting transfers between devices: 43.8 us -> none  [passed_along(): return lax.ppermute(block, axis, route)]
    reduce_scatter x6 -> x0, waiting for transfers between devices: 39.4 us -> none  [visit(): lax.psum_scatter(text_grad, 'pair', scatter_dimension=0, tiled=True)]
    all_gather x1 -> x0, waiting for transfers between devices: 24.5 us -> none  [body(): text_now = lax.all_gather(text_emb, 'pair', axis=0, tiled=True)]
    add x6 -> x0, other arithmetic: 7.64 us -> none  [the longest x5 7.64 us: body(): partial_value = text_grad if offset == 0 else partial_value + text_grad]
    unnamed x48 -> x4, local copies, waits for them, and re-layouts: 7.78 us -> 3.69 us
  transfers between devices with their start and end apart: 18 -> 0, of which waited for: 13 -> 0; matrix products, arithmetic and copies ran while one was open for 14% -> 0% of each run, Pallas kernels for 0% -> 0%
where the time goes in v2:
time: 79.7 us; the launch traced here: 78.6 us
  Pallas kernels  71.6 us (90%)
  local copies, waits for them, and re-layouts  4.99 us (6%)
  between operations  1.93 us (2%)
    pallas_call x1, Pallas kernels, body(): pl.pallas_call(functools.partial(kernel, n_blk), out_shape=(jax.ShapeDtyp...  71.6 us
    unnamed x4, local copies, waits for them, and re-layouts  3.69 us

profile of v2, /device:TPU:27, one launch (start us, length us, event | category | flops | bytes accessed | tf_op | source)
XLA Modules:
  0.0 78.6 jit_solution(5071546785839268014)
XLA Ops:
  1.9 71.6 %shard_map.67 = (f32[8,448]{1,0:T(8,128)}, f32[448,768]{1,0:T(8,128)}, f32[448,768]{1,0:T(8,128)}) custom-call(bf16[448,768]{1,0:T(8,128)(2,1)} %images_ref.1, bf16[448,768]{1,0:T(8,128)(2,1)} %texts_ref.1, f32[1]{0:T(128)} %bitcast.3.scale_ref, f32[1]{0:T(128)} %bitcast.4.bias_ref), custom_call_target="tpu_custom_call" | custom-call | tf_op jit(solution)/shard_map/pallas_call | solution.py:387
  73.6 1.3 %slice.3 = f32[1,448]{1,0:T(1,128)} slice(f32[8,448]{1,0:T(8,128)} %get-tuple-element.6), slice={[0:1], [0:448]} | slice | bytes 3584 | tf_op jit(solution)/shard_map/slice | solution.py:421
  74.9 0.0 copy-start
  74.9 2.6 %copy.11 = f32[448,768]{1,0:T(8,128)} copy(f32[448,768]{1,0:T(8,128)} %get-tuple-element.13) | data formatting | bytes 2752512
  77.5 0.0 copy-done
  77.5 1.1 %copy.12 = f32[448,768]{1,0:T(8,128)} copy(f32[448,768]{1,0:T(8,128)S(1)} %copy-done) | data formatting | bytes 2752512
Async XLA Ops:
  74.9 2.6 %copy-start = (f32[448,768]{1,0:T(8,128)S(1)}, f32[448,768]{1,0:T(8,128)}, u32[]{:S(2)}) copy-start(f32[448,768]{1,0:T(8,128)} %get-tuple-element.14) | copy-start | bytes 4128772
